TPU v7x, 32 devices: a whole 2x2x4 slice. The times are simulated.
32 devices in a mesh: batch: 2 (over core), lon: 4 (over y, x), lat: 4 (over z).
Axes of the slice: x: 2, y: 2, z: 4, core: 2. Of those that a mesh axis runs over, the one named last changes fastest.
Arguments:
- imagery: bfloat16 [6, 512, 4096], P('batch', 'lat', 'lon'), parts along dimension 0, may hold values from -6 to 6
- stem_weight: bfloat16 [4, 768, 1024], replicated, may hold values from -0.109375 to 0.109375
- down_weight: bfloat16 [1024, 512], replicated, may hold values from -0.1875 to 0.1875
- height_qkv: bfloat16 [512, 1024], replicated, may hold values from -0.25 to 0.25
- height_bias: float32 [8, 63], replicated, may hold values from -1.5 to 301.5
- width_qkv: bfloat16 [512, 1024], replicated, may hold values from -0.25 to 0.25
- width_bias: float32 [8, 256], replicated, may hold values from -1.5 to 301.5
- up_weight: bfloat16 [512, 1024], replicated, may hold values from -0.25 to 0.25
Outputs:
- block_output: bfloat16 [64, 256, 1024], P(('batch', 'lat'), 'lon'), parts along dimension 0
There are 2 independent parts, one for each index of `batch`. A program takes and returns all parts, laid end to end along the dimension named above; an argument that names none is the same for every part. Nothing has to cross between parts.
All inputs are finite; a program needn't handle non-finite values.
Results may differ from a plain program's by a relative error of at most 0.012.
Values may be sent and summed in bfloat16 or wider, within the bound.
A program may use at most 128 MiB of HBM per device.

v0:
```python
import jax
import jax.numpy as jnp
from jax import lax
from jax.sharding import PartitionSpec as P

QK = 256
VD = 512
HEADS = 8
PATCH = 16
DQ = 32
DV = 64
lowest_score = -1e30


def extended(cells, sides, width, closed):
    for axis, dim in sides:
        count = lax.axis_size(axis)
        ends = count if closed else count - 1
        head = lax.slice_in_dim(cells, 0, width, axis=dim)
        tail = lax.slice_in_dim(cells, cells.shape[dim] - width, cells.shape[dim], axis=dim)
        cells = jnp.concatenate(
            [
                lax.ppermute(tail, axis, [(i, (i + 1) % count) for i in range(ends)]),
                cells,
                lax.ppermute(head, axis, [((i + 1) % count, i) for i in range(ends)]),
            ],
            axis=dim,
        )
    return cells


def stem_features(padded, stem_weight, map_rows, map_cols):
    channels = padded.shape[0]
    blocks = padded.reshape(channels, map_rows + 1, PATCH, map_cols + 1, PATCH)
    blocks = blocks.transpose(1, 3, 0, 2, 4).reshape(
        map_rows + 1, map_cols + 1, channels * PATCH * PATCH
    )
    summed = jnp.zeros((map_rows * map_cols, stem_weight.shape[2]), jnp.float32)
    for row_shift in range(2):
        for col_shift in range(2):
            window = blocks[row_shift : row_shift + map_rows, col_shift : col_shift + map_cols]
            window = window.reshape(map_rows * map_cols, channels * PATCH * PATCH)
            summed = summed + jnp.dot(
                window, stem_weight[2 * row_shift + col_shift], preferred_element_type=jnp.float32
            )
    return jax.nn.relu(summed).astype(jnp.bfloat16)


def online_update(carried, scores, value_heads, form):
    running_max, denominator, weighted = carried
    new_peak = jnp.maximum(running_max, jnp.max(scores, axis=-1))
    weights = jnp.exp(scores - new_peak[..., None])
    denominator = jnp.sum(weights, axis=-1)
    weighted = jnp.einsum(
        form, weights.astype(jnp.bfloat16), value_heads, preferred_element_type=jnp.float32
    )
    return (new_peak, denominator, weighted)


def on_device(
    imagery, stem_weight, down_weight, height_qkv, height_bias, width_qkv, width_bias, up_weight
):
    rim_width = PATCH // 2
    widened = extended(imagery, (("lon", 2),), rim_width, True)
    padded = extended(widened, (("lat", 1),), rim_width, False)
    map_rows = imagery.shape[1] // PATCH
    map_cols = imagery.shape[2] // PATCH
    full_height = map_rows * lax.axis_size("lat")
    full_width = map_cols * lax.axis_size("lon")
    row_first = lax.axis_index("lat") * map_rows
    col_first = lax.axis_index("lon") * map_cols
    score_scale = DQ ** (-0.5)
    features = stem_features(padded, stem_weight, map_rows, map_cols)
    middle = jax.nn.relu(jnp.dot(features, down_weight, preferred_element_type=jnp.float32)).astype(
        jnp.bfloat16
    )
    height_proj = jnp.dot(middle, height_qkv, preferred_element_type=jnp.float32).astype(
        jnp.bfloat16
    )
    height_proj = height_proj.reshape(map_rows, map_cols, 2 * QK + VD)
    height_queries = height_proj[..., :QK].reshape(map_rows, map_cols, HEADS, DQ)
    initial = (
        jnp.full((HEADS, map_cols, map_rows), lowest_score, jnp.float32),
        jnp.zeros((HEADS, map_cols, map_rows), jnp.float32),
        jnp.zeros((HEADS, map_cols, map_rows, DV), jnp.float32),
    )
    key_rows = lax.all_gather(height_proj[..., QK : 2 * QK], "lat", axis=0, tiled=True)
    value_rows = lax.all_gather(height_proj[..., 2 * QK :], "lat", axis=0, tiled=True)
    key_count = key_rows.shape[0]
    scores = (
        jnp.einsum(
            "pwnd,ownd->nwpo",
            height_queries,
            key_rows.reshape(key_count, map_cols, HEADS, DQ),
            preferred_element_type=jnp.float32,
        )
        * score_scale
    )
    offsets = (
        jnp.arange(key_count, dtype=jnp.int32)[None, :]
        - (row_first + jnp.arange(map_rows, dtype=jnp.int32))[:, None]
        + full_height
        - 1
    )
    scores = scores + jnp.take(height_bias, offsets, axis=1)[:, None]
    running_max, denominator, weighted = online_update(
        initial, scores, value_rows.reshape(key_count, map_cols, HEADS, DV), "nwpo,ownd->nwpd"
    )
    height_out = (
        (weighted / denominator[..., None])
        .transpose(2, 1, 0, 3)
        .reshape(map_rows, map_cols, VD)
        .astype(jnp.bfloat16)
    )
    width_proj = jnp.dot(
        height_out.reshape(map_rows * map_cols, VD), width_qkv, preferred_element_type=jnp.float32
    ).astype(jnp.bfloat16)
    width_proj = width_proj.reshape(map_rows, map_cols, 2 * QK + VD)
    width_queries = width_proj[..., :QK].reshape(map_rows, map_cols, HEADS, DQ)
    width_initial = (
        jnp.full((HEADS, map_rows, map_cols), lowest_score, jnp.float32),
        jnp.zeros((HEADS, map_rows, map_cols), jnp.float32),
        jnp.zeros((HEADS, map_rows, map_cols, DV), jnp.float32),
    )
    key_cols = lax.all_gather(width_proj[..., QK : 2 * QK], "lon", axis=1, tiled=True)
    value_cols = lax.all_gather(width_proj[..., 2 * QK :], "lon", axis=1, tiled=True)
    key_count = key_cols.shape[1]
    scores = (
        jnp.einsum(
            "hwnd,hknd->nhwk",
            width_queries,
            key_cols.reshape(map_rows, key_count, HEADS, DQ),
            preferred_element_type=jnp.float32,
        )
        * score_scale
    )
    offsets = (
        jnp.arange(key_count, dtype=jnp.int32)[None, :]
        - (col_first + jnp.arange(map_cols, dtype=jnp.int32))[:, None]
    ) % full_width
    scores = scores + jnp.take(width_bias, offsets, axis=1)[:, None]
    width_max, width_denominator, width_weighted = online_update(
        width_initial, scores, value_cols.reshape(map_rows, key_count, HEADS, DV), "nhwk,hknd->nhwd"
    )
    width_out = (
        (width_weighted / width_denominator[..., None])
        .transpose(1, 2, 0, 3)
        .reshape(map_rows * map_cols, VD)
        .astype(jnp.bfloat16)
    )
    branch = jnp.dot(jax.nn.relu(width_out), up_weight, preferred_element_type=jnp.float32)
    result = jax.nn.relu(features.astype(jnp.float32) + branch).astype(jnp.bfloat16)
    return result.reshape(map_rows, map_cols, up_weight.shape[1])


def solution(mesh):
    placed = (P("batch", "lat", "lon"), P(), P(), P(), P(), P(), P(), P())
    return jax.shard_map(
        on_device,
        mesh=mesh,
        in_specs=placed,
        out_specs=P(("batch", "lat"), "lon", None),
        check_vma=False,
    )
```

profile of v0, /device:TPU:0, one launch (start us, length us, event | category | flops | bytes accessed | tf_op | source)
XLA Modules:
  0.0 249.6 jit_solution(9862370127342275498)
XLA Ops:
  7.7 3.0 %collective-permute-start = (bf16[3,128,8]{2,1,0:T(8,128)(2,1)S(1)}, bf16[3,128,8]{2,1,0:T(8,128)(2,1)S(1)}, u32[]{:S(2)}, u32[]{:S(2)}) collective-permute-start(bf16[3,128,8]{2,1,0:T(8,128)(2,1)S(1)} %get-tuple-element.16), channel_id=1, source_target_pairs={{0,4},{4,8},{8,12},{12,0},{1,5},{5,9},{9,13},{13,1},{2,6},{6,10},{... | collective-permute-start | bytes 18440 | tf_op jit(solution)/shard_map/ppermute | solution.py:23
  11.7 3.4 %collective-permute-done = bf16[3,128,8]{2,1,0:T(8,128)(2,1)S(1)} collective-permute-done((bf16[3,128,8]{2,1,0:T(8,128)(2,1)S(1)}, bf16[3,128,8]{2,1,0:T(8,128)(2,1)S(1)}, u32[]{:S(2)}, u32[]{:S(2)}) %collective-permute-start) | collective-permute-done | bytes 6176 | tf_op jit(solution)/shard_map/ppermute | solution.py:23
  15.1 1.7 collective-permute-done.1
  16.8 1.8 concatenate.6
  18.6 3.5 %collective-permute-start.2 = (bf16[3,8,1040]{2,1,0:T(8,128)(2,1)S(1)}, bf16[3,8,1040]{2,1,0:T(8,128)(2,1)S(1)}, u32[]{:S(2)}, u32[]{:S(2)}) collective-permute-start(bf16[3,8,1040]{2,1,0:T(8,128)(2,1)S(1)} %get-tuple-element.13), channel_id=1, source_target_pairs={{0,1},{1,2},{2,3},{4,5},{5,6},{6,7},{8,9},{9,10},{10,11},{12,13},{... | collective-permute-start | bytes 149768 | tf_op jit(solution)/shard_map/ppermute | solution.py:23
  23.9 4.3 %collective-permute-done.3 = bf16[3,8,1040]{2,1,0:T(8,128)(2,1)S(1)} collective-permute-done((bf16[3,8,1040]{2,1,0:T(8,128)(2,1)S(1)}, bf16[3,8,1040]{2,1,0:T(8,128)(2,1)S(1)}, u32[]{:S(2)}, u32[]{:S(2)}) %collective-permute-start.3) | collective-permute-done | bytes 49952 | tf_op jit(solution)/shard_map/ppermute | solution.py:25
  28.3 6.8 %reshape.225 = bf16[3,9,16,65,16]{4,3,2,1,0:T(8,128)(2,1)} reshape(bf16[3,144,1040]{2,1,0:T(8,128)(2,1)S(1)} %pad_maximum_fusion) | data formatting | bytes 1797120 | tf_op jit(solution)/shard_map/reshape | solution.py:34
  35.0 7.2 %copy.53 = bf16[9,65,3,16,16]{1,4,3,2,0:T(8,128)(2,1)S(1)} copy(bf16[9,65,3,16,16]{4,1,3,0,2:T(8,128)(2,1)} %bitcast.68) | data formatting | bytes 1797120 | tf_op jit(solution)/shard_map/transpose | solution.py:35
  42.2 3.7 %fusion.58 = (bf16[8,64,768]{1,2,0:T(8,128)(2,1)}, bf16[8,64,768]{1,2,0:T(8,128)(2,1)}, bf16[8,64,768]{1,2,0:T(8,128)(2,1)}, bf16[8,64,768]{1,2,0:T(8,128)(2,1)}) fusion(bf16[9,65,768]{1,2,0:T(8,128)(2,1)S(1)} %bitcast.67), kind=kLoop, calls=%fused_computation.83 | loop fusion | bytes 6291456 | tf_op jit(solution)/shard_map/slice | solution.py:41
  45.9 1.8 copy.56
  49.1 3.8 %fusion.19 = f32[512,1024]{1,0:T(8,128)} fusion(bf16[512,768]{1,0:T(8,128)(2,1)S(1)} %bitcast.80, bf16[4,768,1024]{2,1,0:T(8,128)(2,1)} %param.9), kind=kOutput, calls=%fused_computation.26 | convolution fusion | flops 805306368 | bytes 4456448 | tf_op jit(solution)/shard_map/dot_general | solution.py:43
  52.9 3.8 %fusion.21 = f32[512,1024]{1,0:T(8,128)} fusion(bf16[512,768]{1,0:T(8,128)(2,1)S(1)} %bitcast.81, bf16[4,768,1024]{2,1,0:T(8,128)(2,1)} %param.9), kind=kOutput, calls=%fused_computation.28 | convolution fusion | flops 805306368 | bytes 4456448 | tf_op jit(solution)/shard_map/dot_general | solution.py:43
  57.4 3.9 %fusion.23 = f32[512,1024]{1,0:T(8,128)} fusion(bf16[512,768]{1,0:T(8,128)(2,1)S(1)} %bitcast.82, bf16[4,768,1024]{2,1,0:T(8,128)(2,1)} %param.9), kind=kOutput, calls=%fused_computation.30 | convolution fusion | flops 805306368 | bytes 4456448 | tf_op jit(solution)/shard_map/dot_general | solution.py:43
  61.9 4.4 %maximum_convert_fusion.1 = bf16[512,1024]{1,0:T(8,128)(2,1)S(1)} fusion(f32[512,1024]{1,0:T(8,128)} %fusion.19, f32[512,1024]{1,0:T(8,128)} %fusion.23, f32[512,1024]{1,0:T(8,128)} %fusion.21, bf16[512,768]{1,0:T(8,128)(2,1)S(1)} %bitcast.72, bf16[4,768,1024]{2,1,0:T(8,128)(2,1)} %param.9), kind=kOutput, calls=%fused_computation.21 | convolution fusion | flops 807927808 | bytes 9699328 | tf_op jit(solution)/shard_map/dot_general | solution.py:43
  66.3 2.9 %convolution_convert_fusion.1 = bf16[512,1024]{1,0:T(8,128)(2,1)S(1)} fusion(bf16[512,1024]{1,0:T(8,128)(2,1)S(1)} %copy-done, bf16[512,1024]{1,0:T(8,128)(2,1)S(1)} %maximum_convert_fusion.1, bf16[1024,512]{1,0:T(8,128)(2,1)} %param.10), kind=kOutput, calls=%fused_computation.37 | convolution fusion | flops 1074790400 | bytes 4194304 | tf_op jit(solution)/shard_map/dot_general | solution.py:77
  73.2 24.3 %all-gather.5.cloned.1.call-done = bf16[32,64,256]{2,1,0:T(8,128)(2,1)} async-done(((bf16[8,64,256]{2,1,0:T(8,128)(2,1)}), bf16[32,64,256]{2,1,0:T(8,128)(2,1)}) %all-gather.5.cloned.1.call-update) | async-done | bytes 1048592 | tf_op jit(solution)/shard_map/all_gather | solution.py:87
  97.5 2.0 copy.59
  99.5 6.5 %copy.61 = bf16[32,64,8,32]{3,0,1,2:T(8,128)(2,1)} copy(bf16[32,64,8,32]{1,3,2,0:T(8,128)(2,1)S(1)} %bitcast.70) | data formatting | bytes 2097152 | tf_op jit(solution)/shard_map/reshape | solution.py:94
  106.0 4.7 %fusion.13 = (f32[8,64,8]{2,1,0:T(8,128)S(1)}, f32[8,64,8,32]{3,2,1,0:T(8,128)S(1)}) fusion(f32[8,8,32]{2,1,0:T(8,128)S(1)} %select_bitcast_fusion.1, bf16[8,64,8,32]{3,0,1,2:T(8,128)(2,1)S(1)} %copy.60, bf16[32,64,8,32]{3,0,1,2:T(8,128)(2,1)} %copy.61), kind=kOutput, calls=%fused_computation.22 | convolution fusion | flops 8777728 | bytes 1859584 | tf_op jit(solution)/shard_map/pwnd,ownd->nwpo/dot_general | solution.py:91
  112.1 32.4 %all-gather.7.cloned.1.call-done = bf16[32,64,512]{2,1,0:T(8,128)(2,1)} async-done(((bf16[8,64,512]{2,1,0:T(8,128)(2,1)}), bf16[32,64,512]{2,1,0:T(8,128)(2,1)}) %all-gather.7.cloned.1.call-update) | async-done | bytes 2097168 | tf_op jit(solution)/shard_map/all_gather | solution.py:88
  144.5 6.2 %reshape.234 = bf16[32,64,8,64]{3,2,1,0:T(8,128)(2,1)} reshape(bf16[32,64,512]{2,1,0:T(8,128)(2,1)} %all-gather.7.cloned.1.call-done) | data formatting | bytes 4194304 | tf_op jit(solution)/shard_map/reshape | solution.py:107
  150.6 8.5 %fusion.8 = bf16[8,64,8,64]{3,0,1,2:T(8,128)(2,1)S(1)} fusion(bf16[32,64,8,64]{3,2,1,0:T(8,128)(2,1)} %reshape.234, f32[8,64,8,32]{3,2,1,0:T(8,128)S(1)} %get-tuple-element.18, f32[8,64,8]{0,1,2:T(8,128)S(1)} %bitcast.84, f32[8,64,8]{2,1,0:T(8,128)S(1)} %broadcast_maximum_fusion, f32[8,8,32]{2,1,0:T(8,128)S(1)} %select_bitcast_fusion.1), kind=kOutput, calls=%fused_computation.13 | convolution fusion | flops 17825792 | bytes 3186688 | tf_op jit(solution)/shard_map/nwpo,ownd->nwpd/dot_general | solution.py:54
  160.4 1.9 convolution_convert_fusion
  165.1 54.8 %gather_fusion.1 = f32[16384,8]{1,0:T(8,128)} fusion(f32[8,256]{0,1:T(8,128)S(1)} %copy.71, s32[16384]{0:T(1024)S(1)} %broadcast_clamp_fusion), kind=kCustom, calls=%fused_computation.1 | custom fusion | bytes 1114112 | tf_op jit(solution)/shard_map/jit(_take)/gather | solution.py:141
  219.9 5.2 %copy.72 = f32[64,256,8]{1,0,2:T(8,128)S(1)} copy(f32[64,256,8]{2,1,0:T(8,128)} %bitcast.69) | data formatting | bytes 1048576 | tf_op jit(solution)/shard_map/jit(_take)/gather | solution.py:141
  225.5 1.6 copy.68
  228.3 1.9 copy-done.2
  230.2 1.5 fusion.3
  231.7 3.0 %copy.74 = bf16[8,256,512]{1,2,0:T(8,128)(2,1)S(1)} copy(bf16[8,256,512]{2,0,1:T(8,128)(2,1)} %all-gather.11.cloned.1.call-done) | data formatting | bytes 4194304 | tf_op jit(solution)/shard_map/all_gather | solution.py:126
  234.7 3.1 %fusion.36 = bf16[8,64,8,64]{3,1,0,2:T(8,128)(2,1)S(1)} fusion(f32[8,64,8]{1,0,2:T(8,128)S(1)} %bitcast.86, bf16[8,256,8,64]{1,3,2,0:T(8,128)(2,1)S(1)} %bitcast.75, f32[8,8,64,256]{3,2,1,0:T(8,128)} %copy-done.2, f32[8,8,64]{2,1,0:T(8,128)S(1)} %broadcast_maximum_fusion.1, f32[8,64,256]{2,1,0:T(8,128)S(1)} %select_bitcast_fusion), kind=kOutput, calls=%fused_computation.45 | convolution fusion | flops 139198464 | bytes 7372800 | tf_op jit(solution)/shard_map/nhwk,hknd->nhwd/dot_general | solution.py:54
  238.6 1.4 max.37
  240.0 3.1 %maximum_convert_fusion = bf16[512,1024]{1,0:T(8,128)(2,1)} fusion(bf16[512,1024]{1,0:T(8,128)(2,1)S(1)} %copy-done.7, bf16[512,512]{1,0:T(8,128)(2,1)} %max.37, bf16[512,1024]{1,0:T(8,128)(2,1)} %param.15), kind=kOutput, calls=%fused_computation.15 | convolution fusion | flops 538968064 | bytes 3670016 | tf_op jit(solution)/shard_map/dot_general | solution.py:151
  (72 shorter events, 18.3 us)
Async XLA Ops:
  6.5 59.8 %copy-start = (bf16[512,1024]{1,0:T(8,128)(2,1)S(1)}, bf16[512,1024]{1,0:T(8,128)(2,1)}, u32[]{:S(2)}) copy-start(bf16[512,1024]{1,0:T(8,128)(2,1)} %param.11) | copy-start | bytes 3145732
  6.5 90.9 %all-gather.5.cloned.1.call-start = ((), (), s32[]{:S(2)}) async-start(), calls=%async_computation | async-start | bytes 1310720 | tf_op jit(solution)/shard_map/all_gather | solution.py:87
  7.7 7.4 %collective-permute-start = (bf16[3,128,8]{2,1,0:T(8,128)(2,1)S(1)}, bf16[3,128,8]{2,1,0:T(8,128)(2,1)S(1)}, u32[]{:S(2)}, u32[]{:S(2)}) collective-permute-start(bf16[3,128,8]{2,1,0:T(8,128)(2,1)S(1)} %get-tuple-element.16), channel_id=1, source_target_pairs={{0,4},{4,8},{8,12},{12,0},{1,5},{5,9},{9,13},{13,1},{2,6},{6,10},{... | collective-permute-start | bytes 18440 | tf_op jit(solution)/shard_map/ppermute | solution.py:23
  10.7 6.1 %collective-permute-start.1 = (bf16[3,128,8]{2,1,0:T(8,128)(2,1)S(1)}, bf16[3,128,8]{2,1,0:T(8,128)(2,1)S(1)}, u32[]{:S(2)}, u32[]{:S(2)}) collective-permute-start(bf16[3,128,8]{2,1,0:T(8,128)(2,1)S(1)} %get-tuple-element.15), channel_id=1, source_target_pairs={{4,0},{8,4},{12,8},{0,12},{5,1},{9,5},{13,9},{1,13},{6,2},{10,6},{... | collective-permute-start | bytes 18440 | tf_op jit(solution)/shard_map/ppermute | solution.py:25
  18.6 5.3 %collective-permute-start.2 = (bf16[3,8,1040]{2,1,0:T(8,128)(2,1)S(1)}, bf16[3,8,1040]{2,1,0:T(8,128)(2,1)S(1)}, u32[]{:S(2)}, u32[]{:S(2)}) collective-permute-start(bf16[3,8,1040]{2,1,0:T(8,128)(2,1)S(1)} %get-tuple-element.13), channel_id=1, source_target_pairs={{0,1},{1,2},{2,3},{4,5},{5,6},{6,7},{8,9},{9,10},{10,11},{12,13},{... | collective-permute-start | bytes 149768 | tf_op jit(solution)/shard_map/ppermute | solution.py:23
  22.1 6.0 %collective-permute-start.3 = (bf16[3,8,1040]{2,1,0:T(8,128)(2,1)S(1)}, bf16[3,8,1040]{2,1,0:T(8,128)(2,1)S(1)}, u32[]{:S(2)}, u32[]{:S(2)}) collective-permute-start(bf16[3,8,1040]{2,1,0:T(8,128)(2,1)S(1)} %get-tuple-element.14), channel_id=1, source_target_pairs={{1,0},{2,1},{3,2},{5,4},{6,5},{7,6},{9,8},{10,9},{11,10},{13,12},{... | collective-permute-start | bytes 149768 | tf_op jit(solution)/shard_map/ppermute | solution.py:25
  45.9 1.9 copy-start.5
  49.1 3.8 %copy-start.8 = (bf16[8,64,768]{2,1,0:T(8,128)(2,1)S(1)}, bf16[8,64,768]{2,1,0:T(8,128)(2,1)}, u32[]{:S(2)}) copy-start(bf16[8,64,768]{2,1,0:T(8,128)(2,1)} %copy.55) | copy-start | bytes 2359300
  52.9 3.8 %copy-start.4 = (bf16[8,64,768]{1,2,0:T(8,128)(2,1)S(1)}, bf16[8,64,768]{1,2,0:T(8,128)(2,1)}, u32[]{:S(2)}) copy-start(bf16[8,64,768]{1,2,0:T(8,128)(2,1)} %get-tuple-element.8) | copy-start | bytes 2359300
  57.4 3.9 %copy-start.3 = (bf16[8,64,768]{1,2,0:T(8,128)(2,1)S(1)}, bf16[8,64,768]{1,2,0:T(8,128)(2,1)}, u32[]{:S(2)}) copy-start(bf16[8,64,768]{1,2,0:T(8,128)(2,1)} %get-tuple-element.5) | copy-start | bytes 2359300
  66.3 2.9 %copy-start.6 = (bf16[512,1024]{1,0:T(8,128)(2,1)}, bf16[512,1024]{1,0:T(8,128)(2,1)S(1)}, u32[]{:S(2)}) copy-start(bf16[512,1024]{1,0:T(8,128)(2,1)S(1)} %maximum_convert_fusion.1) | copy-start | bytes 3145732
  69.2 2.1 copy-start.10
  70.0 74.5 %all-gather.7.cloned.1.call-start = ((), (), s32[]{:S(2)}) async-start(), calls=%async_computation.1 | async-start | bytes 2621440 | tf_op jit(solution)/shard_map/all_gather | solution.py:88
  70.9 154.6 %all-gather.9.cloned.1.call-start = ((), (), s32[]{:S(2)}) async-start(), calls=%async_computation.2 | async-start | bytes 1310720 | tf_op jit(solution)/shard_map/all_gather | solution.py:125
  162.4 2.6 %copy-start.9 = (f32[8,256]{1,0:T(8,128)S(1)}, f32[8,256]{1,0:T(8,128)}, u32[]{:S(2)}) copy-start(f32[8,256]{1,0:T(8,128)} %param.14) | copy-start | bytes 24580
  163.3 68.4 %all-gather.11.cloned.1.call-start = ((), (), s32[]{:S(2)}) async-start(), calls=%async_computation.3 | async-start | bytes 2621440 | tf_op jit(solution)/shard_map/all_gather | solution.py:126
  228.3 1.9 copy-start.2
  237.9 2.2 copy-start.7
  238.6 4.5 %copy-start.1 = (bf16[512,1024]{1,0:T(8,128)(2,1)S(1)}, bf16[512,1024]{1,0:T(8,128)(2,1)}, u32[]{:S(2)}) copy-start(bf16[512,1024]{1,0:T(8,128)(2,1)} %param.11) | copy-start | bytes 3145732
Sparse Core Ops, SparseCore 0:
  70.1 27.2 all-gather.4
  99.0 45.3 all-gather.6
  163.5 25.3 all-gather.8
  190.6 35.2 all-gather.10
where the time goes:
time: 250 us
  local copies, waits for them, and re-layouts  116 us (46%)
  waiting for transfers between devices  66.6 us (27%)
  matrix products  41.2 us (16%)
  between operations  13.5 us (5%)
  starting transfers between devices  9.32 us (4%)
  other arithmetic  3.35 us (1%)
    gather x2, local copies, waits for them, and re-layouts, on_device(): scores = scores + jnp.take(width_bias, offsets, axis=1)[:, None]  59.9 us
    all_gather x1, waiting for transfers between devices, on_device(): lax.all_gather(height_proj[..., 2 * QK:], 'lat', axis=0, tiled=True)  32.4 us
    all_gather x1, waiting for transfers between devices, on_device(): lax.all_gather(height_proj[..., QK:2 * QK], 'lat', axis=0, tiled=True)  24.3 us
    dot_general x4, matrix products, stem_features(): jnp.dot(window, stem_weight[2 * row_shift + col_shift], preferred_element...  15.8 us
    dot_general x2, matrix products, online_update(): jnp.einsum(form, weights.astype(jnp.bfloat16), value_heads, preferred_ele...  11.6 us
    slice x5, local copies, waits for them, and re-layouts, stem_features(): blocks[row_shift:row_shift + map_rows, col_shift:col_shift + map_cols]  8.17 us
    transpose x1, local copies, waits for them, and re-layouts, stem_features(): blocks.transpose(1, 3, 0, 2, 4)  7.16 us
    reshape x1, local copies, waits for them, and re-layouts, stem_features(): blocks = padded.reshape(channels, map_rows + 1, PATCH, map_cols + 1, PATCH)  6.77 us
  transfers between devices with their start and end apart: 8, of which 6 were waited for; matrix products, arithmetic and copies ran while one was open for 33% of the time, Pallas kernels for 0%

commit v1 on v0

--- a/solution.py
+++ b/solution.py
@@ -1,7 +1,9 @@
+import functools
 import jax
 import jax.numpy as jnp
 from jax import lax
 from jax.sharding import PartitionSpec as P
+from jax.lax import axis_index, axis_size, ppermute
 
 QK = 256
 VD = 512
@@ -10,6 +12,25 @@
 DQ = 32
 DV = 64
 lowest_score = -1e30
+
+
+def manage_columns(slab_in, chip_axis, in_dim):
+    local_part = axis_size(chip_axis)
+    big = axis_index(chip_axis)
+    part_next, x_next = (local_part, big)
+    high, e_now = (slab_in, 1)
+    while e_now < part_next:
+        z2 = ppermute(
+            high, axis_name=chip_axis, perm=[(src_i, src_i ^ e_now) for src_i in range(part_next)]
+        )
+        state_now = jnp.concatenate([high, z2], in_dim)
+        mixed_arr = jnp.concatenate([z2, high], axis=in_dim)
+        high = jnp.where(x_next & e_now == 0, state_now, mixed_arr)
+        e_now = 2 * e_now
+    return high
+
+
+_push_cube = functools.partial(manage_columns, chip_axis="lat", in_dim=0)
 
 
 def extended(cells, sides, width, closed):
@@ -85,7 +106,7 @@
         jnp.zeros((HEADS, map_cols, map_rows, DV), jnp.float32),
     )
     key_rows = lax.all_gather(height_proj[..., QK : 2 * QK], "lat", axis=0, tiled=True)
-    value_rows = lax.all_gather(height_proj[..., 2 * QK :], "lat", axis=0, tiled=True)
+    value_rows = _push_cube(height_proj[..., 2 * QK :])
     key_count = key_rows.shape[0]
     scores = (
         jnp.einsum(

time: 250 us -> 264 us (1.056)
  other arithmetic: 3.35 us -> 11.7 us
  waiting for transfers between devices: 66.6 us -> 70.3 us
  starting transfers between devices: 9.32 us -> 12.8 us
  matrix products: 41.2 us -> 38.5 us
    ppermute x0 -> x2, waiting for transfers between devices: none -> 60.3 us  [manage_columns(): ppermute(high, axis_name=chip_axis, perm=[(src_i, src_i ^ e_now) for src_...]
    all_gather x1 -> x0, waiting for transfers between devices: 32.4 us -> none  [on_device(): lax.all_gather(height_proj[..., 2 * QK:], 'lat', axis=0, tiled=True)]
    all_gather x1, waiting for transfers between devices: 24.3 us -> 0.01 us  [on_device(): lax.all_gather(height_proj[..., QK:2 * QK], 'lat', axis=0, tiled=True)]
    select_n x0 -> x3, other arithmetic: none -> 8.32 us  [manage_columns(): high = jnp.where(x_next & e_now == 0, state_now, mixed_arr)]
    concatenate x0 -> x3, local copies, waits for them, and re-layouts: none -> 6.95 us  [manage_columns(): state_now = jnp.concatenate([high, z2], in_dim)]
    reshape x1 -> x0, local copies, waits for them, and re-layouts: 6.17 us -> none  [on_device(): value_rows.reshape(key_count, map_cols, HEADS, DV)]
    ppermute x0 -> x2, starting transfers between devices: none -> 3.97 us  [manage_columns(): ppermute(high, axis_name=chip_axis, perm=[(src_i, src_i ^ e_now) for src_...]
    dot_general x2, matrix products: 11.6 us -> 8.95 us  [online_update(): jnp.einsum(form, weights.astype(jnp.bfloat16), value_heads, preferred_ele...]
  transfers between devices with their start and end apart: 8 -> 9, of which waited for: 6 -> 6; matrix products, arithmetic and copies ran while one was open for 33% -> 32% of each run, Pallas kernels for 0% -> 0%
where the time goes in v1:
time: 264 us
  local copies, waits for them, and re-layouts  117 us (44%)
  waiting for transfers between devices  70.3 us (27%)
  matrix products  38.5 us (15%)
  between operations  13.5 us (5%)
  starting transfers between devices  12.8 us (5%)
  other arithmetic  11.7 us (4%)
    ppermute x2, waiting for transfers between devices, manage_columns(): ppermute(high, axis_name=chip_axis, perm=[(src_i, src_i ^ e_now) for src_...  60.3 us
    gather x2, local copies, waits for them, and re-layouts, on_device(): scores = scores + jnp.take(width_bias, offsets, axis=1)[:, None]  60.1 us
    dot_general x4, matrix products, stem_features(): jnp.dot(window, stem_weight[2 * row_shift + col_shift], preferred_element...  15.8 us
    dot_general x2, matrix products, online_update(): jnp.einsum(form, weights.astype(jnp.bfloat16), value_heads, preferred_ele...  8.95 us
    select_n x3, other arithmetic, manage_columns(): high = jnp.where(x_next & e_now == 0, state_now, mixed_arr)  8.32 us
    slice x5, local copies, waits for them, and re-layouts, stem_features(): blocks[row_shift:row_shift + map_rows, col_shift:col_shift + map_cols]  8.14 us
    transpose x1, local copies, waits for them, and re-layouts, stem_features(): blocks.transpose(1, 3, 0, 2, 4)  7.16 us
    concatenate x3, local copies, waits for them, and re-layouts, manage_columns(): state_now = jnp.concatenate([high, z2], in_dim)  6.95 us
  transfers between devices with their start and end apart: 9, of which 6 were waited for; matrix products, arithmetic and copies ran while one was open for 32% of the time, Pallas kernels for 0%

profile of v1, /device:TPU:0, one launch (start us, length us, event | category | flops | bytes accessed | tf_op | source)
XLA Modules:
  0.0 263.7 jit_solution(10256018806202555361)
XLA Ops:
  7.7 3.0 %collective-permute-start = (bf16[3,128,8]{2,1,0:T(8,128)(2,1)S(1)}, bf16[3,128,8]{2,1,0:T(8,128)(2,1)S(1)}, u32[]{:S(2)}, u32[]{:S(2)}) collective-permute-start(bf16[3,128,8]{2,1,0:T(8,128)(2,1)S(1)} %get-tuple-element.16), channel_id=1, source_target_pairs={{0,4},{4,8},{8,12},{12,0},{1,5},{5,9},{9,13},{13,1},{2,6},{6,10},{... | collective-permute-start | bytes 18440 | tf_op jit(solution)/shard_map/ppermute | solution.py:44
  11.7 3.4 %collective-permute-done = bf16[3,128,8]{2,1,0:T(8,128)(2,1)S(1)} collective-permute-done((bf16[3,128,8]{2,1,0:T(8,128)(2,1)S(1)}, bf16[3,128,8]{2,1,0:T(8,128)(2,1)S(1)}, u32[]{:S(2)}, u32[]{:S(2)}) %collective-permute-start) | collective-permute-done | bytes 6176 | tf_op jit(solution)/shard_map/ppermute | solution.py:44
  15.1 1.7 collective-permute-done.1
  16.8 1.8 concatenate.32
  18.6 3.5 %collective-permute-start.2 = (bf16[3,8,1040]{2,1,0:T(8,128)(2,1)S(1)}, bf16[3,8,1040]{2,1,0:T(8,128)(2,1)S(1)}, u32[]{:S(2)}, u32[]{:S(2)}) collective-permute-start(bf16[3,8,1040]{2,1,0:T(8,128)(2,1)S(1)} %get-tuple-element.13), channel_id=1, source_target_pairs={{0,1},{1,2},{2,3},{4,5},{5,6},{6,7},{8,9},{9,10},{10,11},{12,13},{... | collective-permute-start | bytes 149768 | tf_op jit(solution)/shard_map/ppermute | solution.py:44
  23.9 4.3 %collective-permute-done.3 = bf16[3,8,1040]{2,1,0:T(8,128)(2,1)S(1)} collective-permute-done((bf16[3,8,1040]{2,1,0:T(8,128)(2,1)S(1)}, bf16[3,8,1040]{2,1,0:T(8,128)(2,1)S(1)}, u32[]{:S(2)}, u32[]{:S(2)}) %collective-permute-start.3) | collective-permute-done | bytes 49952 | tf_op jit(solution)/shard_map/ppermute | solution.py:46
  28.3 6.8 %reshape.231 = bf16[3,9,16,65,16]{4,3,2,1,0:T(8,128)(2,1)} reshape(bf16[3,144,1040]{2,1,0:T(8,128)(2,1)S(1)} %pad_maximum_fusion) | data formatting | bytes 1797120 | tf_op jit(solution)/shard_map/reshape | solution.py:55
  35.0 7.2 %copy.53 = bf16[9,65,3,16,16]{1,4,3,2,0:T(8,128)(2,1)S(1)} copy(bf16[9,65,3,16,16]{4,1,3,0,2:T(8,128)(2,1)} %bitcast.68) | data formatting | bytes 1797120 | tf_op jit(solution)/shard_map/transpose | solution.py:56
  42.2 3.6 %fusion.58 = (bf16[8,64,768]{1,2,0:T(8,128)(2,1)}, bf16[8,64,768]{1,2,0:T(8,128)(2,1)}, bf16[8,64,768]{1,2,0:T(8,128)(2,1)}, bf16[8,64,768]{1,2,0:T(8,128)(2,1)}) fusion(bf16[9,65,768]{1,2,0:T(8,128)(2,1)S(1)} %bitcast.67), kind=kLoop, calls=%fused_computation.86 | loop fusion | bytes 6291456 | tf_op jit(solution)/shard_map/slice | solution.py:62
  45.8 1.8 copy.56
  49.1 3.8 %fusion.19 = f32[512,1024]{1,0:T(8,128)} fusion(bf16[512,768]{1,0:T(8,128)(2,1)S(1)} %bitcast.80, bf16[4,768,1024]{2,1,0:T(8,128)(2,1)} %param.9), kind=kOutput, calls=%fused_computation.28 | convolution fusion | flops 805306368 | bytes 4456448 | tf_op jit(solution)/shard_map/dot_general | solution.py:64
  52.9 3.8 %fusion.21 = f32[512,1024]{1,0:T(8,128)} fusion(bf16[512,768]{1,0:T(8,128)(2,1)S(1)} %bitcast.81, bf16[4,768,1024]{2,1,0:T(8,128)(2,1)} %param.9), kind=kOutput, calls=%fused_computation.30 | convolution fusion | flops 805306368 | bytes 4456448 | tf_op jit(solution)/shard_map/dot_general | solution.py:64
  57.4 3.8 %fusion.23 = f32[512,1024]{1,0:T(8,128)} fusion(bf16[512,768]{1,0:T(8,128)(2,1)S(1)} %bitcast.82, bf16[4,768,1024]{2,1,0:T(8,128)(2,1)} %param.9), kind=kOutput, calls=%fused_computation.32 | convolution fusion | flops 805306368 | bytes 4456448 | tf_op jit(solution)/shard_map/dot_general | solution.py:64
  61.9 4.4 %maximum_convert_fusion.1 = bf16[512,1024]{1,0:T(8,128)(2,1)S(1)} fusion(f32[512,1024]{1,0:T(8,128)} %fusion.19, f32[512,1024]{1,0:T(8,128)} %fusion.23, f32[512,1024]{1,0:T(8,128)} %fusion.21, bf16[512,768]{1,0:T(8,128)(2,1)S(1)} %bitcast.72, bf16[4,768,1024]{2,1,0:T(8,128)(2,1)} %param.9), kind=kOutput, calls=%fused_computation.23 | convolution fusion | flops 807927808 | bytes 9699328 | tf_op jit(solution)/shard_map/dot_general | solution.py:64
  66.3 2.9 %convolution_convert_fusion.1 = bf16[512,1024]{1,0:T(8,128)(2,1)S(1)} fusion(bf16[512,1024]{1,0:T(8,128)(2,1)S(1)} %copy-done, bf16[512,1024]{1,0:T(8,128)(2,1)S(1)} %maximum_convert_fusion.1, bf16[1024,512]{1,0:T(8,128)(2,1)} %param.10), kind=kOutput, calls=%fused_computation.39 | convolution fusion | flops 1074790400 | bytes 4194304 | tf_op jit(solution)/shard_map/dot_general | solution.py:98
  71.7 9.2 %collective-permute-done.4 = bf16[8,64,512]{2,1,0:T(8,128)(2,1)S(1)} collective-permute-done((bf16[8,64,512]{2,1,0:T(8,128)(2,1)S(1)}, bf16[8,64,512]{2,1,0:T(8,128)(2,1)S(1)}, u32[]{:S(2)}, u32[]{:S(2)}) %collective-permute-start.4) | collective-permute-done | bytes 524320 | tf_op jit(solution)/shard_map/ppermute | solution.py:23
  82.1 2.3 collective-permute-start.5
  90.5 2.4 maximum_select_fusion.1
  92.9 51.2 %collective-permute-done.5 = bf16[16,64,512]{2,1,0:T(8,128)(2,1)} collective-permute-done((bf16[16,64,512]{2,1,0:T(8,128)(2,1)}, bf16[16,64,512]{2,1,0:T(8,128)(2,1)}, u32[]{:S(2)}, u32[]{:S(2)}) %collective-permute-start.5) | collective-permute-done | bytes 1048608 | tf_op jit(solution)/shard_map/ppermute | solution.py:23
  144.1 3.9 %concatenate.40 = bf16[16,64,8,64]{3,2,1,0:T(8,128)(2,1)} reshape(bf16[16,64,512]{2,1,0:T(8,128)(2,1)} %collective-permute-done.5) | data formatting | bytes 2097152 | tf_op jit(solution)/shard_map/concatenate | solution.py:26
  148.0 4.7 %maximum_select_fusion = bf16[32,64,8,64]{3,2,1,0:T(8,128)(2,1)} fusion(bf16[16,64,8,64]{3,2,1,0:T(8,128)(2,1)} %concatenate.40, bf16[16,64,8,64]{3,2,1,0:T(8,128)(2,1)S(1)} %maximum_select_fusion.1, pred[]{:T(512)S(6)} %eq.8), kind=kLoop, calls=%fused_computation.2 | loop fusion | flops 3145728 | bytes 4194305 | tf_op jit(solution)/shard_map/jit(_where)/select_n | solution.py:28
  152.7 2.0 copy.59
  154.8 6.6 %copy.61 = bf16[32,64,8,32]{3,0,1,2:T(8,128)(2,1)} copy(bf16[32,64,8,32]{1,3,2,0:T(8,128)(2,1)S(1)} %bitcast.70) | data formatting | bytes 2097152 | tf_op jit(solution)/shard_map/reshape | solution.py:115
  161.3 4.7 %fusion.13 = (f32[8,64,8]{2,1,0:T(8,128)S(1)}, f32[8,64,8,32]{3,2,1,0:T(8,128)S(1)}) fusion(f32[8,8,32]{2,1,0:T(8,128)S(1)} %select_bitcast_fusion.1, bf16[8,64,8,32]{3,0,1,2:T(8,128)(2,1)S(1)} %copy-done.8, bf16[32,64,8,32]{3,0,1,2:T(8,128)(2,1)} %copy.61), kind=kOutput, calls=%fused_computation.24 | convolution fusion | flops 8777728 | bytes 1859584 | tf_op jit(solution)/shard_map/pwnd,ownd->nwpo/dot_general | solution.py:112
  167.4 5.8 %fusion.8 = bf16[8,64,8,64]{3,0,1,2:T(8,128)(2,1)S(1)} fusion(bf16[32,64,8,64]{3,2,1,0:T(8,128)(2,1)S(1)} %copy-done.7, f32[8,64,8,32]{3,2,1,0:T(8,128)S(1)} %get-tuple-element.18, f32[8,64,8]{0,1,2:T(8,128)S(1)} %bitcast.84, f32[8,64,8]{2,1,0:T(8,128)S(1)} %broadcast_maximum_fusion, f32[8,8,32]{2,1,0:T(8,128)S(1)} %select_bitcast_fusion.1), kind=kOutput, calls=%fused_computation.15 | convolution fusion | flops 17825792 | bytes 3186688 | tf_op jit(solution)/shard_map/nwpo,ownd->nwpd/dot_general | solution.py:75
  174.5 1.9 convolution_convert_fusion
  179.0 55.0 %gather_fusion.1 = f32[16384,8]{1,0:T(8,128)} fusion(f32[8,256]{0,1:T(8,128)S(1)} %copy.71, s32[16384]{0:T(1024)S(1)} %broadcast_clamp_fusion), kind=kCustom, calls=%fused_computation.1 | custom fusion | bytes 1114112 | tf_op jit(solution)/shard_map/jit(_take)/gather | solution.py:162
  233.9 5.2 %copy.72 = f32[64,256,8]{1,0,2:T(8,128)S(1)} copy(f32[64,256,8]{2,1,0:T(8,128)} %bitcast.69) | data formatting | bytes 1048576 | tf_op jit(solution)/shard_map/jit(_take)/gather | solution.py:162
  242.3 1.9 copy-done.2
  245.8 3.0 %copy.74 = bf16[8,256,512]{1,2,0:T(8,128)(2,1)S(1)} copy(bf16[8,256,512]{2,0,1:T(8,128)(2,1)} %all-gather.8.cloned.1.call-done) | data formatting | bytes 4194304 | tf_op jit(solution)/shard_map/all_gather | solution.py:147
  248.8 3.1 %fusion.36 = bf16[8,64,8,64]{3,1,0,2:T(8,128)(2,1)S(1)} fusion(f32[8,64,8]{1,0,2:T(8,128)S(1)} %bitcast.86, bf16[8,256,8,64]{1,3,2,0:T(8,128)(2,1)S(1)} %bitcast.75, f32[8,8,64,256]{3,2,1,0:T(8,128)} %copy-done.2, f32[8,8,64]{2,1,0:T(8,128)S(1)} %broadcast_maximum_fusion.1, f32[8,64,256]{2,1,0:T(8,128)S(1)} %select_bitcast_fusion), kind=kOutput, calls=%fused_computation.48 | convolution fusion | flops 139198464 | bytes 7372800 | tf_op jit(solution)/shard_map/nhwk,hknd->nhwd/dot_general | solution.py:75
  254.1 3.1 %maximum_convert_fusion = bf16[512,1024]{1,0:T(8,128)(2,1)} fusion(bf16[512,1024]{1,0:T(8,128)(2,1)S(1)} %copy-done.10, bf16[512,512]{1,0:T(8,128)(2,1)} %max.37, bf16[512,1024]{1,0:T(8,128)(2,1)} %param.15), kind=kOutput, calls=%fused_computation.17 | convolution fusion | flops 538968064 | bytes 3670016 | tf_op jit(solution)/shard_map/dot_general | solution.py:172
  (84 shorter events, 28.5 us)
Async XLA Ops:
  6.5 59.8 %copy-start = (bf16[512,1024]{1,0:T(8,128)(2,1)S(1)}, bf16[512,1024]{1,0:T(8,128)(2,1)}, u32[]{:S(2)}) copy-start(bf16[512,1024]{1,0:T(8,128)(2,1)} %param.11) | copy-start | bytes 3145732
  6.5 146.2 %all-gather.4.cloned.1.call-start = ((), (), s32[]{:S(2)}) async-start(), calls=%async_computation | async-start | bytes 1310720 | tf_op jit(solution)/shard_map/all_gather | solution.py:108
  7.7 7.4 %collective-permute-start = (bf16[3,128,8]{2,1,0:T(8,128)(2,1)S(1)}, bf16[3,128,8]{2,1,0:T(8,128)(2,1)S(1)}, u32[]{:S(2)}, u32[]{:S(2)}) collective-permute-start(bf16[3,128,8]{2,1,0:T(8,128)(2,1)S(1)} %get-tuple-element.16), channel_id=1, source_target_pairs={{0,4},{4,8},{8,12},{12,0},{1,5},{5,9},{9,13},{13,1},{2,6},{6,10},{... | collective-permute-start | bytes 18440 | tf_op jit(solution)/shard_map/ppermute | solution.py:44
  10.7 6.1 %collective-permute-start.1 = (bf16[3,128,8]{2,1,0:T(8,128)(2,1)S(1)}, bf16[3,128,8]{2,1,0:T(8,128)(2,1)S(1)}, u32[]{:S(2)}, u32[]{:S(2)}) collective-permute-start(bf16[3,128,8]{2,1,0:T(8,128)(2,1)S(1)} %get-tuple-element.15), channel_id=1, source_target_pairs={{4,0},{8,4},{12,8},{0,12},{5,1},{9,5},{13,9},{1,13},{6,2},{10,6},{... | collective-permute-start | bytes 18440 | tf_op jit(solution)/shard_map/ppermute | solution.py:46
  18.6 5.3 %collective-permute-start.2 = (bf16[3,8,1040]{2,1,0:T(8,128)(2,1)S(1)}, bf16[3,8,1040]{2,1,0:T(8,128)(2,1)S(1)}, u32[]{:S(2)}, u32[]{:S(2)}) collective-permute-start(bf16[3,8,1040]{2,1,0:T(8,128)(2,1)S(1)} %get-tuple-element.13), channel_id=1, source_target_pairs={{0,1},{1,2},{2,3},{4,5},{5,6},{6,7},{8,9},{9,10},{10,11},{12,13},{... | collective-permute-start | bytes 149768 | tf_op jit(solution)/shard_map/ppermute | solution.py:44
  22.1 6.0 %collective-permute-start.3 = (bf16[3,8,1040]{2,1,0:T(8,128)(2,1)S(1)}, bf16[3,8,1040]{2,1,0:T(8,128)(2,1)S(1)}, u32[]{:S(2)}, u32[]{:S(2)}) collective-permute-start(bf16[3,8,1040]{2,1,0:T(8,128)(2,1)S(1)} %get-tuple-element.14), channel_id=1, source_target_pairs={{1,0},{2,1},{3,2},{5,4},{6,5},{7,6},{9,8},{10,9},{11,10},{13,12},{... | collective-permute-start | bytes 149768 | tf_op jit(solution)/shard_map/ppermute | solution.py:46
  45.8 1.9 copy-start.5
  49.1 3.8 %copy-start.11 = (bf16[8,64,768]{2,1,0:T(8,128)(2,1)S(1)}, bf16[8,64,768]{2,1,0:T(8,128)(2,1)}, u32[]{:S(2)}) copy-start(bf16[8,64,768]{2,1,0:T(8,128)(2,1)} %copy.55) | copy-start | bytes 2359300
  52.9 3.8 %copy-start.4 = (bf16[8,64,768]{1,2,0:T(8,128)(2,1)S(1)}, bf16[8,64,768]{1,2,0:T(8,128)(2,1)}, u32[]{:S(2)}) copy-start(bf16[8,64,768]{1,2,0:T(8,128)(2,1)} %get-tuple-element.8) | copy-start | bytes 2359300
  57.4 3.9 %copy-start.3 = (bf16[8,64,768]{1,2,0:T(8,128)(2,1)S(1)}, bf16[8,64,768]{1,2,0:T(8,128)(2,1)}, u32[]{:S(2)}) copy-start(bf16[8,64,768]{1,2,0:T(8,128)(2,1)} %get-tuple-element.5) | copy-start | bytes 2359300
  66.3 2.9 %copy-start.9 = (bf16[512,1024]{1,0:T(8,128)(2,1)}, bf16[512,1024]{1,0:T(8,128)(2,1)S(1)}, u32[]{:S(2)}) copy-start(bf16[512,1024]{1,0:T(8,128)(2,1)S(1)} %maximum_convert_fusion.1) | copy-start | bytes 3145732
  69.2 15.4 %copy-start.13 = (f32[8,63]{1,0:T(8,128)S(1)}, f32[8,63]{1,0:T(8,128)}, u32[]{:S(2)}) copy-start(f32[8,63]{1,0:T(8,128)} %param.12) | copy-start | bytes 6052
  69.2 11.7 %collective-permute-start.4 = (bf16[8,64,512]{2,1,0:T(8,128)(2,1)S(1)}, bf16[8,64,512]{2,1,0:T(8,128)(2,1)S(1)}, u32[]{:S(2)}, u32[]{:S(2)}) collective-permute-start(bf16[8,64,512]{2,1,0:T(8,128)(2,1)S(1)} %slice.84), channel_id=1, source_target_pairs={{0,1},{1,0},{2,3},{3,2},{4,5},{5,4},{6,7},{7,6},{8,9},{9,8},{10,11... | collective-permute-start | bytes 1572872 | tf_op jit(solution)/shard_map/ppermute | solution.py:23
  71.7 167.9 %all-gather.6.cloned.1.call-start = ((), (), s32[]{:S(2)}) async-start(), calls=%async_computation.1 | async-start | bytes 1310720 | tf_op jit(solution)/shard_map/all_gather | solution.py:146
  82.1 62.0 %collective-permute-start.5 = (bf16[16,64,512]{2,1,0:T(8,128)(2,1)}, bf16[16,64,512]{2,1,0:T(8,128)(2,1)}, u32[]{:S(2)}, u32[]{:S(2)}) collective-permute-start(bf16[16,64,512]{2,1,0:T(8,128)(2,1)} %maximum_select_fusion.2), channel_id=1, source_target_pairs={{0,2},{1,3},{2,0},{3,1},{4,6},{5,7},{6,4},{7,5},{8,10},{9,11},{10,... | collective-permute-start | bytes 3145736 | tf_op jit(solution)/shard_map/ppermute | solution.py:23
  87.1 3.4 %copy-start.6 = (bf16[8,64,8,64]{3,2,1,0:T(8,128)(2,1)S(1)}, bf16[8,64,8,64]{3,2,1,0:T(8,128)(2,1)}, u32[]{:S(2)}) copy-start(bf16[8,64,8,64]{3,2,1,0:T(8,128)(2,1)} %concatenate.34) | copy-start | bytes 1572868
  154.7 6.6 %copy-start.8 = (bf16[8,64,8,32]{3,0,1,2:T(8,128)(2,1)S(1)}, bf16[8,64,8,32]{3,0,1,2:T(8,128)(2,1)}, u32[]{:S(2)}) copy-start(bf16[8,64,8,32]{3,0,1,2:T(8,128)(2,1)} %copy.60) | copy-start | bytes 786436
  161.3 6.1 %copy-start.7 = (bf16[32,64,8,64]{3,2,1,0:T(8,128)(2,1)S(1)}, bf16[32,64,8,64]{3,2,1,0:T(8,128)(2,1)}, u32[]{:S(2)}) copy-start(bf16[32,64,8,64]{3,2,1,0:T(8,128)(2,1)} %maximum_select_fusion) | copy-start | bytes 6291460
  176.5 2.3 copy-start.12
  177.4 68.4 %all-gather.8.cloned.1.call-start = ((), (), s32[]{:S(2)}) async-start(), calls=%async_computation.2 | async-start | bytes 2621440 | tf_op jit(solution)/shard_map/all_gather | solution.py:147
  242.3 1.9 copy-start.2
  251.9 2.2 copy-start.10
  252.7 4.5 %copy-start.1 = (bf16[512,1024]{1,0:T(8,128)(2,1)S(1)}, bf16[512,1024]{1,0:T(8,128)(2,1)}, u32[]{:S(2)}) copy-start(bf16[512,1024]{1,0:T(8,128)(2,1)} %param.11) | copy-start | bytes 3145732
Sparse Core Ops, SparseCore 0:
  71.8 58.1 all-gather.3
  177.5 25.6 all-gather.5
  205.1 35.2 all-gather.7
